TPU v7x, 32 devices: a whole 2x2x4 slice. The times are simulated.
32 devices in a mesh: grp: 2 (over x), cell: 16 (over z, y, core).
Axes of the slice: x: 2, y: 2, z: 4, core: 2. Of those that a mesh axis runs over, the one named last changes fastest.
Arguments:
- counts: bfloat16 [65536, 2560], P(('grp', 'cell')), parts along dimension 0, may hold values from 0.0099487305 to 4
- cell_init: float32 [64, 65536], P(None, ('grp', 'cell')), parts along dimension 1, may hold values from 0.1 to 1
- load_init: float32 [64, 5120], P(None, ('grp', 'cell')), parts along dimension 1, may hold values from 0.1 to 1
- band_offsets: int32 [512, 3], P(('grp', 'cell')), parts along dimension 0, may hold values from -2 to 2
- band_weights: bfloat16 [512, 3, 128, 128], P(('grp', 'cell')), parts along dimension 0, may hold values from 0.049804688 to 1
Outputs:
- cell_factors: float32 [64, 65536], P(None, ('grp', 'cell')), parts along dimension 1
- gene_loadings: float32 [64, 5120], P(None, ('grp', 'cell')), parts along dimension 1
- fit_error: float32 [65536], P(('grp', 'cell')), parts along dimension 0
There are 2 independent parts, one for each index of `grp`. A program takes and returns all parts, laid end to end along the dimension named above; each array names one. Nothing has to cross between parts.
Inputs may be any that keep to these rules, and one draw needn't show every extreme that they name: `band_offsets`: cell block b couples to cell block b plus this offset; blocks outside the slab hold zero factors.
All inputs are finite; a program needn't handle non-finite values.
Results may differ from a plain program's by a relative error of at most 0.0003.
Values may be sent and summed in bfloat16 or wider, within the bound.
A program may use at most 64 MiB of HBM per device.

v0:
```python
import jax
import jax.numpy as jnp
from jax import lax
from jax.sharding import PartitionSpec as P

ITERS = 2


graph_weight = 0.5
epsilon = 1e-09


def extended(cells, sides, width):
    for axis, dim in sides:
        count = lax.axis_size(axis)
        ends = count - 1
        head = lax.slice_in_dim(cells, 0, width, axis=dim)
        tail = lax.slice_in_dim(cells, cells.shape[dim] - width, cells.shape[dim], axis=dim)
        cells = jnp.concatenate(
            [
                lax.ppermute(tail, axis, [(i, (i + 1) % count) for i in range(ends)]),
                cells,
                lax.ppermute(head, axis, [((i + 1) % count, i) for i in range(ends)]),
            ],
            axis=dim,
        )
    return cells


def make_gene_rows(counts, fact_half):
    return lax.dot_general(
        counts, fact_half, (((0,), (1,)), ((), ())), preferred_element_type=jnp.float32
    )


def body(counts, cell_init, load_init, band_offsets, band_weights):
    highest = lax.Precision.HIGHEST
    factors = cell_init
    loadings = load_init
    rank = factors.shape[0]
    nblocks = band_weights.shape[0]
    block = band_weights.shape[-1]
    degree = jnp.sum(band_weights.astype(jnp.float32), axis=(1, 3)).reshape(-1)
    positions = jnp.arange(nblocks, dtype=jnp.int32)[:, None] + 2 + band_offsets
    load_half = loadings.astype(jnp.bfloat16)
    for sweep in range(ITERS):
        fact_half = factors.astype(jnp.bfloat16)
        local_gram = jnp.dot(factors, factors.T, precision=highest)
        own_sums = lax.psum_scatter(
            make_gene_rows(counts, fact_half), "cell", scatter_dimension=0, tiled=True
        )
        factor_gram = lax.psum(local_gram, "cell")
        loadings = (
            loadings * own_sums.T / (jnp.dot(factor_gram, loadings, precision=highest) + epsilon)
        )
        load_gram = lax.psum(jnp.dot(loadings, loadings.T, precision=highest), "cell")
        load_half = lax.all_gather(loadings.astype(jnp.bfloat16), "cell", axis=1, tiled=True)
        data_term = lax.dot_general(
            load_half, counts, (((1,), (1,)), ((), ())), preferred_element_type=jnp.float32
        )
        padded = extended(fact_half, (("cell", 1),), 2 * block)
        blocks = padded.reshape(rank, nblocks + 4, block)
        picked = jnp.take(blocks, positions, axis=1)
        result = jnp.einsum(
            "nsij,knsj->kni", band_weights, picked, preferred_element_type=jnp.float32
        )
        graph_term = result.reshape(rank, nblocks * block)
        numer = data_term + graph_weight * graph_term
        denom = (
            jnp.dot(load_gram, factors, precision=highest)
            + graph_weight * degree[None, :] * factors
            + epsilon
        )
        factors = factors * numer / denom
    fact_half = factors.astype(jnp.bfloat16)
    recon = lax.dot_general(
        fact_half, load_half, (((0,), (0,)), ((), ())), preferred_element_type=jnp.float32
    )
    fit_error = jnp.mean(jnp.square(counts.astype(jnp.float32) - recon), axis=1)
    return (factors, loadings, fit_error)


def solution(mesh):
    in_specs = (
        P(("grp", "cell"), None),
        P(None, ("grp", "cell")),
        P(None, ("grp", "cell")),
        P(("grp", "cell"), None),
        P(("grp", "cell"), None, None, None),
    )
    out_specs = (P(None, ("grp", "cell")), P(None, ("grp", "cell")), P(("grp", "cell")))
    return jax.shard_map(body, mesh=mesh, in_specs=in_specs, out_specs=out_specs, check_vma=False)
```

profile of v0, /device:TPU:0, one launch (start us, length us, event | category | flops | bytes accessed | tf_op | source)
XLA Modules:
  0.0 354.8 jit_solution(14617937835609833320)
XLA Ops:
  7.2 0.0 copy-start.1
  7.2 0.0 copy-start.4
  7.2 0.0 copy-start
  7.2 0.0 reduce-scatter.7.cloned.1.call-start
  7.2 1.2 convert_element_type.21
  8.5 9.2 %fusion.30 = f32[2560,64]{1,0:T(8,128)} fusion(bf16[64,2048]{1,0:T(8,128)(2,1)S(1)} %convert_element_type.21, bf16[2048,2560]{1,0:T(8,128)(2,1)} %param.7), kind=kOutput, calls=%fused_computation.57 | convolution fusion | flops 671088640 | bytes 11403264
  17.7 0.0 reduce-scatter.7.cloned.1.call-update
  17.7 0.0 reduce-scatter.9.cloned.1.call-start
  17.8 1.3 collective-permute-start.1
  19.1 3.0 collective-permute-start
  22.1 0.0 copy-done.4
  22.1 0.0 copy-done
  22.1 0.3 convert_reduce_fusion
  22.5 0.1 copy.28
  22.6 0.1 reshape.63
  22.7 0.0 copy-done.1
  22.7 0.6 fusion.26
  23.3 0.1 copy.27
  23.4 62.7 %psum.28 = f32[64,64]{1,0:T(8,128)S(1)} all-reduce(f32[64,64]{1,0:T(8,128)S(1)} %fusion.26), channel_id=1, replica_groups=mesh['grp'=2,'cell'=16] {'cell'}, use_global_device_ids=true, to_apply=%region_1.0 | all-reduce | flops 4096 | bytes 32768 | tf_op jit(solution)/shard_map/psum | solution.py:52
  86.1 0.0 collective-permute-done.1
  86.1 0.0 collective-permute-done
  86.1 0.1 copy_bitcast_fusion.1
  86.2 0.7 gather_fusion
  86.9 0.8 fusion.8
  87.7 0.0 reduce-scatter.7.cloned.1.call-done
  87.7 1.0 copy.39
  88.7 1.1 fusion.11
  89.8 0.0 copy-start.2
  89.9 0.2 fusion.27
  90.1 0.4 copy-done.2
  90.5 18.7 %all-gather = bf16[16,160,64]{1,2,0:T(8,128)(2,1)S(1)} all-gather(bf16[1,160,64]{1,2,0:T(8,128)(2,1)S(1)} %convert_bitcast_fusion.1), channel_id=1, replica_groups=mesh['grp'=2,'cell'=16] {'cell'}, dimensions={0}, use_global_device_ids=true | all-gather | bytes 348160 | tf_op jit(solution)/shard_map/all_gather | solution.py:57
  109.1 0.3 copy.26
  109.4 1.5 reshape.60
  110.9 59.9 %psum.29 = f32[64,64]{1,0:T(8,128)S(1)} all-reduce(f32[64,64]{1,0:T(8,128)S(1)} %fusion.27), channel_id=1, replica_groups=mesh['grp'=2,'cell'=16] {'cell'}, use_global_device_ids=true, to_apply=%region_2.4 | all-reduce | flops 4096 | bytes 32768 | tf_op jit(solution)/shard_map/psum | solution.py:56
  170.8 7.4 %fusion.5 = f32[64,2048]{1,0:T(8,128)S(1)} fusion(f32[64,2048]{1,0:T(8,128)S(1)} %copy-done.1, bf16[2560,64]{0,1:T(8,128)(2,1)} %reshape.60, bf16[2048,2560]{1,0:T(8,128)(2,1)} %param.7, f32[16,8,8,128]{3,2,1,0:T(8,128)S(1)} %fusion.8), kind=kOutput, calls=%fused_computation.14 | convolution fusion | flops 671350784 | bytes 12386304 | tf_op jit(solution)/shard_map/dot_general | solution.py:58
  178.1 0.7 fusion.25
  178.8 5.9 %convolution_bitcast_fusion = f32[2560,64]{0,1:T(8,128)S(1)} fusion(bf16[64,2048]{1,0:T(8,128)(2,1)S(1)} %get-tuple-element.10, bf16[2048,2560]{1,0:T(8,128)(2,1)} %param.7), kind=kOutput, calls=%fused_computation.3 | convolution fusion | flops 671088640 | bytes 11403264 | tf_op jit(solution)/shard_map/dot_general | solution.py:31
  184.7 1.5 copy.40
  186.2 0.0 reduce-scatter.9.cloned.1.call-update
  186.2 1.3 collective-permute-start.3
  187.5 3.2 collective-permute-start.2
  190.7 0.6 fusion.28
  191.3 58.4 %psum.30 = f32[64,64]{1,0:T(8,128)} all-reduce(f32[64,64]{1,0:T(8,128)S(1)} %fusion.28), channel_id=1, replica_groups=mesh['grp'=2,'cell'=16] {'cell'}, use_global_device_ids=true, to_apply=%region_5.7 | all-reduce | flops 4096 | bytes 32768 | tf_op jit(solution)/shard_map/psum | solution.py:52
  249.7 0.0 collective-permute-done.3
  249.7 0.0 collective-permute-done.2
  249.7 0.1 copy_bitcast_fusion
  249.8 0.7 gather_fusion.1
  250.5 0.8 fusion.9
  251.3 0.0 reduce-scatter.9.cloned.1.call-done
  251.3 1.0 copy.41
  252.3 1.1 fusion.10
  253.4 0.0 copy-start.3
  253.5 0.2 fusion.29
  253.7 18.7 %all-gather.1 = bf16[16,160,64]{1,2,0:T(8,128)(2,1)S(1)} all-gather(bf16[1,160,64]{1,2,0:T(8,128)(2,1)S(1)} %convert_bitcast_fusion), channel_id=1, replica_groups=mesh['grp'=2,'cell'=16] {'cell'}, dimensions={0}, use_global_device_ids=true | all-gather | bytes 348160 | tf_op jit(solution)/shard_map/all_gather | solution.py:57
  272.4 0.3 copy.31
  272.7 0.7 reshape.62
  273.4 59.9 %psum.31 = f32[64,64]{1,0:T(8,128)S(1)} all-reduce(f32[64,64]{1,0:T(8,128)S(1)} %fusion.29), channel_id=1, replica_groups=mesh['grp'=2,'cell'=16] {'cell'}, use_global_device_ids=true, to_apply=%region_6.8 | all-reduce | flops 4096 | bytes 32768 | tf_op jit(solution)/shard_map/psum | solution.py:56
  333.3 7.2 %fusion.4 = f32[64,2048]{1,0:T(8,128)S(1)} fusion(f32[64,2048]{1,0:T(8,128)S(1)} %get-tuple-element.11, bf16[2560,64]{0,1:T(8,128)(2,1)S(1)} %reshape.62, bf16[2048,2560]{1,0:T(8,128)(2,1)} %param.7, f32[16,8,8,128]{3,2,1,0:T(8,128)S(1)} %fusion.9), kind=kOutput, calls=%fused_computation.12 | convolution fusion | flops 671350784 | bytes 12386304 | tf_op jit(solution)/shard_map/dot_general | solution.py:58
  340.5 0.6 fusion.3
  341.2 0.0 copy-start.5
  341.2 6.1 %multiply_reduce_fusion = f32[2048]{0:T(1024)S(1)} fusion(bf16[2048,2560]{1,0:T(8,128)(2,1)} %param.7, bf16[2560,64]{0,1:T(8,128)(2,1)S(1)} %reshape.62, f32[64,2048]{1,0:T(8,128)S(1)} %fusion.3), kind=kOutput, calls=%fused_computation.2 | convolution fusion | flops 692189184 | bytes 11345920 | tf_op jit(solution)/shard_map/dot_general | solution.py:76
  347.3 0.0 copy-done.3
  347.3 0.0 copy-done.5
  347.4 0.6 broadcast_multiply_fusion
  (8 shorter events, 0.0 us)
Async XLA Ops:
  7.2 15.5 %copy-start.1 = (f32[64,2048]{1,0:T(8,128)S(1)}, f32[64,2048]{1,0:T(8,128)}, u32[]{:S(2)}) copy-start(f32[64,2048]{1,0:T(8,128)} %param.8) | copy-start | bytes 1572868
  7.2 14.9 %copy-start.4 = (s32[16,3]{0,1:T(4,128)S(1)}, s32[16,3]{0,1:T(4,128)}, u32[]{:S(2)}) copy-start(s32[16,3]{0,1:T(4,128)} %param.10) | copy-start | bytes 580
  7.2 15.0 %copy-start = (bf16[16,3,128,128]{3,2,1,0:T(8,128)(2,1)S(1)}, bf16[16,3,128,128]{3,2,1,0:T(8,128)(2,1)}, u32[]{:S(2)}) copy-start(bf16[16,3,128,128]{3,2,1,0:T(8,128)(2,1)} %param.11) | copy-start | bytes 4718596
  7.2 80.5 %reduce-scatter.7.cloned.1.call-start = ((), (), s32[]{:S(2)}) async-start(), calls=%async_computation.2 | async-start | bytes 1392640
  17.7 233.6 %reduce-scatter.9.cloned.1.call-start = ((), (), s32[]{:S(2)}) async-start(), calls=%async_computation.3 | async-start | bytes 1392640
  17.8 68.3 %collective-permute-start.1 = (bf16[64,256]{1,0:T(8,128)(2,1)S(1)}, bf16[64,256]{1,0:T(8,128)(2,1)S(1)}, u32[]{:S(2)}, u32[]{:S(2)}) collective-permute-start(bf16[64,256]{1,0:T(8,128)(2,1)S(1)} %get-tuple-element.9), channel_id=1, source_target_pairs={{1,0},{2,1},{3,2},{4,3},{5,4},{6,5},{7,6},{8,7},{9,8},{10,9},{11,1... | collective-permute-start | bytes 98312 | tf_op jit(solution)/shard_map/ppermute | solution.py:23
  19.1 67.0 %collective-permute-start = (bf16[64,256]{1,0:T(8,128)(2,1)S(1)}, bf16[64,256]{1,0:T(8,128)(2,1)S(1)}, u32[]{:S(2)}, u32[]{:S(2)}) collective-permute-start(bf16[64,256]{1,0:T(8,128)(2,1)S(1)} %get-tuple-element.8), channel_id=1, source_target_pairs={{0,1},{1,2},{2,3},{3,4},{4,5},{5,6},{6,7},{7,8},{8,9},{9,10},{10,1... | collective-permute-start | bytes 98312 | tf_op jit(solution)/shard_map/ppermute | solution.py:21
  89.8 0.6 copy-start.2
  186.2 63.5 %collective-permute-start.3 = (bf16[64,256]{1,0:T(8,128)(2,1)S(1)}, bf16[64,256]{1,0:T(8,128)(2,1)S(1)}, u32[]{:S(2)}, u32[]{:S(2)}) collective-permute-start(bf16[64,256]{1,0:T(8,128)(2,1)S(1)} %get-tuple-element.7), channel_id=1, source_target_pairs={{1,0},{2,1},{3,2},{4,3},{5,4},{6,5},{7,6},{8,7},{9,8},{10,9},{11,1... | collective-permute-start | bytes 98312 | tf_op jit(solution)/shard_map/ppermute | solution.py:23
  187.5 62.2 %collective-permute-start.2 = (bf16[64,256]{1,0:T(8,128)(2,1)S(1)}, bf16[64,256]{1,0:T(8,128)(2,1)S(1)}, u32[]{:S(2)}, u32[]{:S(2)}) collective-permute-start(bf16[64,256]{1,0:T(8,128)(2,1)S(1)} %get-tuple-element.6), channel_id=1, source_target_pairs={{0,1},{1,2},{2,3},{3,4},{4,5},{5,6},{6,7},{7,8},{8,9},{9,10},{10,1... | collective-permute-start | bytes 98312 | tf_op jit(solution)/shard_map/ppermute | solution.py:21
  253.4 93.9 %copy-start.3 = (f32[64,160]{1,0:T(8,128)}, f32[64,160]{1,0:T(8,128)S(1)}, u32[]{:S(2)}) copy-start(f32[64,160]{1,0:T(8,128)S(1)} %fusion.10) | copy-start | bytes 122884
  341.2 6.2 %copy-start.5 = (f32[64,2048]{1,0:T(8,128)}, f32[64,2048]{1,0:T(8,128)S(1)}, u32[]{:S(2)}) copy-start(f32[64,2048]{1,0:T(8,128)S(1)} %fusion.3) | copy-start | bytes 1572868
Sparse Core Ops, SparseCore 0:
  17.8 61.2 reduce-scatter.6
  186.3 55.7 reduce-scatter.8
where the time goes:
time: 355 us
  blocking collectives  278 us (78%)
  matrix products  42.6 us (12%)
  between operations  14.4 us (4%)
  starting transfers between devices  8.91 us (3%)
  local copies, waits for them, and re-layouts  8.32 us (2%)
    psum x2, blocking collectives, body(): factor_gram = lax.psum(local_gram, 'cell')  121 us
    psum x2, blocking collectives, body(): lax.psum(jnp.dot(loadings, loadings.T, precision=highest), 'cell')  120 us
    all_gather x2, blocking collectives, body(): lax.all_gather(loadings.astype(jnp.bfloat16), 'cell', axis=1, tiled=True)  37.4 us
    dot_general x2, matrix products, body(): lax.dot_general(load_half, counts, (((1,), (1,)), ((), ())), preferred_el...  14.6 us
    unnamed x1, matrix products  9.22 us
  transfers between devices with their start and end apart: 6, of which 0 were waited for; matrix products, arithmetic and copies ran while one was open for 1% of the time, Pallas kernels for 0%

commit v1 on v0

--- a/solution.py
+++ b/solution.py
@@ -1,6 +1,10 @@
+import functools
+
 import jax
 import jax.numpy as jnp
 from jax import lax
+from jax.experimental import pallas as pl
+from jax.experimental.pallas import tpu as pltpu
 from jax.sharding import PartitionSpec as P
 
 ITERS = 2
@@ -8,6 +12,418 @@
 
 graph_weight = 0.5
 epsilon = 1e-09
+MESH = pl.DeviceIdType.MESH
+f32 = jnp.float32
+bf16 = jnp.bfloat16
+ORDER = (2, 1, 3, 0)
+LANES = 128
+
+
+def lanes_of(shape):
+    return lax.broadcasted_iota(jnp.int32, shape, len(shape) - 1)
+
+
+def roll(x, shift):
+    shift %= x.shape[-1]
+    return pltpu.roll(x, shift, x.ndim - 1) if shift else x
+
+
+def pack_chunk(v):
+    tiles = [v[:, LANES * t : LANES * (t + 1)] for t in range(5)]
+    lane = lanes_of((64, LANES))
+    small = lanes_of((16, LANES))
+    pieces = []
+    for p in range(4):
+        first = tiles[p] if p == 0 else roll(jnp.where(lane >= 32 * p, tiles[p], tiles[p + 1]), -32 * p)
+        pieces.append(jnp.concatenate([first, pack_rest(tiles[p + 1], 32 * p, small)], axis=0))
+    return pieces
+
+
+def pack_rest(tile, at, small):
+    rest = roll(tile[0:16], -at)
+    for j in range(1, 4):
+        rest = jnp.where(small >= 32 * j, roll(tile[16 * j : 16 * j + 16], 32 * j - at), rest)
+    return rest
+
+
+def unpack_chunk(pieces):
+    lane = lanes_of((64, LANES))
+    firsts = [roll(x[0:64], 32 * p) for p, x in enumerate(pieces)]
+    rests = [
+        jnp.concatenate([roll(x[64:80], 32 * p - 32 * j) for j in range(4)], axis=0)
+        for p, x in enumerate(pieces)
+    ]
+    tiles = []
+    for t in range(5):
+        tile = None
+        if t >= 1:
+            tile = jnp.where(lane >= 32 * (t - 1), rests[t - 1], firsts[t - 1])
+        if t < 4:
+            tile = firsts[0] if t == 0 else jnp.where(lane >= 32 * t, firsts[t], tile)
+        tiles.append(tile)
+    return tiles
+
+
+def unpack_piece(x):
+    rest = jnp.concatenate([roll(x[64:80], -32 * j) for j in range(4)], axis=0)
+    rest = jnp.where(lanes_of((64, LANES)) < 32, rest, 0.0)
+    return jnp.concatenate([x[0:64], rest], axis=1)
+
+
+def pack_piece(v):
+    return jnp.concatenate(
+        [v[:, 0:LANES], pack_rest(v[:, LANES : 2 * LANES], 0, lanes_of((16, LANES)))], axis=0
+    )
+
+
+def halves(x):
+    hi = x.astype(bf16)
+    return hi, (x - hi.astype(f32)).astype(bf16)
+
+
+def dot_t(a, b):
+    return lax.dot_general(a, b, (((1,), (1,)), ((), ())), preferred_element_type=f32)
+
+
+def dot(a, b):
+    return jnp.dot(a, b, preferred_element_type=f32)
+
+
+def packed_gram(x):
+    full = dot_t(x, x)
+    q = full[0:64] + full[64:128]
+    q = q + roll(q, 64)
+    return jnp.where(lanes_of((32, LANES)) < 64, q[0:32], q[32:64])
+
+
+def gram_operand(s):
+    turned = roll(s, 64)
+    low = lanes_of((32, LANES)) < 64
+    twice = jnp.concatenate([jnp.where(low, s, turned), jnp.where(low, turned, s)], axis=0)
+    hi, lo = halves(twice)
+    return jnp.concatenate([hi, lo], axis=1)
+
+
+def kernel(
+    n, offs, counts, cell_init, load_init, weights, factors_out, load_out, fit_out,
+    cbuf, wbuf, fcur, xf, fb0, fb1, lcur, lhf, dt, gt, deg, csq,
+    fg_own, fg_got, fg_sum, fg_sib, lg_own, lg_got, lg_sum, lg_sib,
+    a_buf, a_got, b_buf, b_got, c_buf, c_got, lh_all,
+    csem, wsem, halo_s, halo_r, g_s, g_r, gs_s, gs_r,
+    a_s, a_r, b_s, b_r, c_s, c_r, l_s, l_r, ls_s, ls_r,
+):
+    me = lax.axis_index("cell")
+    core = lax.rem(me, 2)
+    y = lax.rem(lax.div(me, 2), 2)
+    z = lax.div(me, 4)
+    sib = me + 1 - 2 * core
+    ynb = me + 2 - 4 * y
+    line = lax.div(me, 2)
+    nline = n // 2
+    nb = weights.shape[0]
+    fbs = (fb0, fb1)
+
+    barrier = pltpu.get_barrier_semaphore()
+    for j in range(1, n):
+        pl.semaphore_signal(barrier, inc=1, device_id={"cell": lax.rem(me + j, n)}, device_id_type=MESH)
+
+    width = 640
+    chunk_at = [pl.multiple_of(lax.rem(z + o, n // 4) * width, width) for o in ORDER]
+    ccopies = []
+    for i in range(4):
+        cp = pltpu.make_async_copy(
+            counts.at[:, pl.ds(chunk_at[i], width)], cbuf.at[:, pl.ds(chunk_at[i], width)], csem.at[i]
+        )
+        cp.start()
+        ccopies.append(cp)
+    wcopy = pltpu.make_async_copy(weights, wbuf, wsem)
+    wcopy.start()
+
+    lcur[...] = jnp.zeros_like(lcur)
+    lcur[:, 0:160] = load_init[...]
+    sends = []
+
+    def push(src, dst, ssem, rsem, dev):
+        cp = pltpu.make_async_remote_copy(
+            src_ref=src, dst_ref=dst, send_sem=ssem, recv_sem=rsem, device_id={"cell": dev}, device_id_type=MESH
+        )
+        cp.start()
+        sends.append(cp)
+        return cp
+
+    def set_factors(it, b, value):
+        at = pl.multiple_of(b * LANES, LANES)
+        hi, lo = halves(value)
+        xf[0:64, pl.ds(at, LANES)] = hi
+        xf[64:128, pl.ds(at, LANES)] = lo
+        if it < ITERS:
+            fbs[it][b + 2] = hi
+
+    def first_factors(b, carry):
+        set_factors(0, b, cell_init[:, pl.ds(pl.multiple_of(b * LANES, LANES), LANES)])
+        return carry
+
+    lax.fori_loop(0, nb, first_factors, 0)
+    pl.semaphore_wait(barrier, n - 1)
+
+    def halo(it, go):
+        fb = fbs[it]
+        left = pltpu.make_async_remote_copy(
+            src_ref=fb.at[pl.ds(2, 2)], dst_ref=fb.at[pl.ds(nb + 2, 2)], send_sem=halo_s.at[it, 0],
+            recv_sem=halo_r.at[it, 0], device_id={"cell": lax.rem(me + n - 1, n)}, device_id_type=MESH,
+        )
+        right = pltpu.make_async_remote_copy(
+            src_ref=fb.at[pl.ds(nb, 2)], dst_ref=fb.at[pl.ds(0, 2)], send_sem=halo_s.at[it, 1],
+            recv_sem=halo_r.at[it, 1], device_id={"cell": lax.rem(me + 1, n)}, device_id_type=MESH,
+        )
+        if go == "start":
+            @pl.when(me > 0)
+            def _():
+                left.start()
+
+            @pl.when(me < n - 1)
+            def _():
+                right.start()
+
+            @pl.when(me == 0)
+            def _():
+                fb[0:2] = jnp.zeros((2, 64, LANES), bf16)
+
+            @pl.when(me == n - 1)
+            def _():
+                fb[nb + 2 : nb + 4] = jnp.zeros((2, 64, LANES), bf16)
+        elif go == "recv":
+            @pl.when(me < n - 1)
+            def _():
+                left.wait_recv()
+
+            @pl.when(me > 0)
+            def _():
+                right.wait_recv()
+        else:
+            @pl.when(me > 0)
+            def _():
+                left.wait_send()
+
+            @pl.when(me < n - 1)
+            def _():
+                right.wait_send()
+
+    def gram_start(k, it, own, got, x):
+        own[it] = packed_gram(x)
+        return [
+            push(own.at[it], got.at[it, j - 1], g_s.at[k, it, j - 1], g_r.at[k, it, j - 1],
+                 2 * lax.rem(line + j, nline) + core)
+            for j in range(1, nline)
+        ]
+
+    def gram_middle(k, it, copies, own, got, total, far):
+        acc = own[it]
+        for j, cp in enumerate(copies):
+            cp.wait_recv()
+            acc = acc + got[it, j]
+        total[it] = acc
+        return push(total.at[it], far.at[it], gs_s.at[k, it], gs_r.at[k, it], sib)
+
+    def gram_end(it, copy, total, far):
+        copy.wait_recv()
+        return gram_operand(total[it] + far[it])
+
+    def graph(it, start, stop):
+        fb = fbs[it]
+
+        def step(b, carry):
+            acc = jnp.zeros((80, LANES), f32)
+            for s in range(3):
+                picked = fb[b + 2 + offs[b, s]]
+                lhs = jnp.concatenate([picked, jnp.ones((16, LANES), bf16)], axis=0)
+                acc = acc + dot_t(lhs, wbuf[b, s])
+            gt[b] = graph_weight * acc[0:64]
+            if it == 0:
+                deg[b] = graph_weight * acc[64:72]
+            return carry
+
+        lax.fori_loop(start, stop, step, 0, unroll=2)
+
+    def squares(start, stop):
+        def step(b, carry):
+            rows = pl.ds(pl.multiple_of(b * LANES, LANES), LANES)
+            acc = jnp.zeros((LANES, LANES), f32)
+            for t in range(cbuf.shape[1] // LANES):
+                c = cbuf[rows, LANES * t : LANES * (t + 1)].astype(f32)
+                acc = acc + c * c
+            hi, lo = halves(acc)
+            ones = jnp.ones((16, LANES), bf16)
+            csq[b] = (dot_t(ones, hi) + dot_t(ones, lo))[0:8]
+            return carry
+
+        lax.fori_loop(start, stop, step, 0)
+
+    for it in range(ITERS):
+        last = it == ITERS - 1
+        halo(it, "start")
+        fgc = gram_start(0, it, fg_own, fg_got, xf[...])
+
+        acopies, bcopies, ccs = [], [], []
+
+        def reduce_core(i):
+            acopies[i].wait_recv()
+            b_buf[it, i] = a_buf[it, i, core] + a_got[it, i]
+            bcopies.append(push(b_buf.at[it, i, 1 - y], b_got.at[it, i], b_s.at[it, i], b_r.at[it, i], ynb))
+
+        def reduce_y(i):
+            bcopies[i].wait_recv()
+            c_buf[it, i] = b_buf[it, i, y] + b_got[it, i]
+            if i < 3:
+                dev = 4 * lax.rem(z + ORDER[i], 4) + 2 * y + core
+                ccs.append(push(c_buf.at[it, i], c_got.at[it, i], c_s.at[it, i], c_r.at[it, i], dev))
+
+        fgm = None
+        for i in range(4):
+            if it == 0:
+                ccopies[i].wait()
+            v = dot(xf[0:64, :], cbuf[:, pl.ds(chunk_at[i], width)])
+            for p, piece in enumerate(pack_chunk(v)):
+                a_buf[it, i, p % 2, p // 2] = piece
+            acopies.append(
+                push(a_buf.at[it, i, 1 - core], a_got.at[it, i], a_s.at[it, i], a_r.at[it, i], sib)
+            )
+            if i >= 1:
+                reduce_core(i - 1)
+            if i >= 2:
+                reduce_y(i - 2)
+            if i == 2:
+                fgm = gram_middle(0, it, fgc, fg_own, fg_got, fg_sum, fg_sib)
+        if it == 0:
+            wcopy.wait()
+        halo(it, "recv")
+        graph(it, 0, nb // 4)
+        reduce_core(3)
+        reduce_y(2)
+        graph(it, nb // 4, nb // 2)
+        reduce_y(3)
+        fg = gram_end(it, fgm, fg_sum, fg_sib)
+        own = lcur[...]
+        lhi, llo = halves(own)
+        under = dot(fg, jnp.concatenate([lhi, llo, lhi, llo], axis=0)) + epsilon
+        sums = c_buf[it, 3]
+        for i in range(3):
+            ccs[i].wait_recv()
+            sums = sums + c_got[it, i]
+        own = own * unpack_piece(sums) / under
+        lcur[...] = own
+        lh_all[it, me] = pack_piece(own).astype(bf16)
+        lcs = [
+            push(lh_all.at[it, me], lh_all.at[it, me], l_s.at[it, j - 1], l_r.at[it, j - 1],
+                 2 * lax.rem(line + j, nline) + core)
+            for j in range(1, nline)
+        ]
+        sibs = [push(lh_all.at[it, me], lh_all.at[it, me], ls_s.at[it, 0], ls_r.at[it, 0], sib)]
+        lhi, llo = halves(own)
+        lgc = gram_start(1, it, lg_own, lg_got, jnp.concatenate([lhi, llo], axis=0))
+        if last:
+            load_out[...] = own[:, 0:160]
+        graph(it, nb // 2, nb)
+        for j in range(1, nline):
+            at = 2 * lax.rem(line + nline - j, nline) + core
+            pltpu.make_async_remote_copy(
+                src_ref=lh_all.at[it, at], dst_ref=lh_all.at[it, at], send_sem=l_s.at[it, j - 1],
+                recv_sem=l_r.at[it, j - 1], device_id={"cell": at}, device_id_type=MESH,
+            ).wait_recv()
+            sibs.append(push(lh_all.at[it, at], lh_all.at[it, at], ls_s.at[it, j], ls_r.at[it, j], sib))
+        if last:
+            squares(0, nb)
+        for cp in sibs:
+            cp.wait_recv()
+        for c in range(n // 4):
+            pieces = [lh_all[it, 4 * c + p].astype(f32) for p in range(4)]
+            for t, tile in enumerate(unpack_chunk(pieces)):
+                at = width * c + LANES * t
+                lhf[:, at : at + LANES] = tile.astype(bf16)
+
+        def data(i, carry):
+            rows = pl.ds(pl.multiple_of(i * 256, 256), 256)
+            part = dot_t(lhf[...], cbuf[rows, :])
+            dt[2 * i] = part[:, 0:LANES]
+            dt[2 * i + 1] = part[:, LANES:]
+            return carry
+
+        lax.fori_loop(0, nb // 4, data, 0)
+        lgm = gram_middle(1, it, lgc, lg_own, lg_got, lg_sum, lg_sib)
+        lax.fori_loop(nb // 4, nb // 2, data, 0)
+        lg = gram_end(it, lgm, lg_sum, lg_sib)
+        if last:
+            twice = dot_t(lhf[...], jnp.concatenate([lhf[...], lhf[...]], axis=0))
+            mhi, mlo = halves(twice)
+            pair = jnp.where(lanes_of((64, LANES)) < 64, mhi.astype(f32), mlo.astype(f32)).astype(bf16)
+
+        source = cell_init if it == 0 else fcur
+        target = factors_out if last else fcur
+
+        def update(b, carry):
+            cols = pl.ds(pl.multiple_of(b * LANES, LANES), LANES)
+            f = source[:, cols]
+            x = xf[:, cols]
+            under = dot(lg, jnp.concatenate([x, x], axis=0)) + deg[b][0:1] * f + epsilon
+            new = f * (dt[b] + gt[b]) / under
+            target[:, cols] = new
+            if last:
+                hi = new.astype(bf16)
+                recon2 = dot(pair, jnp.concatenate([hi, hi], axis=0))
+                inner = jnp.sum(hi.astype(f32) * (recon2 - 2.0 * dt[b]), axis=0, keepdims=True)
+                fit_out[pl.ds(b, 1), :] = (csq[b][0:1] + inner) * (1.0 / cbuf.shape[1])
+            else:
+                set_factors(it + 1, b, new)
+            return carry
+
+        lax.fori_loop(0, nb, update, 0, unroll=2)
+
+    for cp in sends:
+        cp.wait_send()
+    for it in range(ITERS):
+        halo(it, "send")
+
+
+def fused(n, counts, cell_init, load_init, band_offsets, band_weights):
+    cells, genes = counts.shape
+    nb = band_weights.shape[0]
+    T = ITERS
+    V = pltpu.VMEM
+    D = pltpu.SemaphoreType.DMA
+    scratch = [
+        V((cells, genes), bf16), V(band_weights.shape, bf16), V((64, cells), f32), V((128, cells), bf16),
+        V((nb + 4, 64, 128), bf16), V((nb + 4, 64, 128), bf16), V((64, 256), f32), V((64, genes), bf16),
+        V((nb, 64, 128), f32), V((nb, 64, 128), f32), V((nb, 8, 128), f32), V((nb, 8, 128), f32),
+    ]
+    for _ in range(2):
+        scratch += [V((T, 32, 128), f32), V((T, n // 2 - 1, 32, 128), f32), V((T, 32, 128), f32), V((T, 32, 128), f32)]
+    scratch += [
+        V((T, 4, 2, 2, 80, 128), f32), V((T, 4, 2, 80, 128), f32),
+        V((T, 4, 2, 80, 128), f32), V((T, 4, 80, 128), f32),
+        V((T, 4, 80, 128), f32), V((T, 3, 80, 128), f32),
+        V((T, n, 80, 128), bf16),
+        D((4,)), D(()), D((T, 2)), D((T, 2)),
+        D((2, T, n // 2 - 1)), D((2, T, n // 2 - 1)), D((2, T)), D((2, T)),
+        D((T, 4)), D((T, 4)), D((T, 4)), D((T, 4)), D((T, 3)), D((T, 3)),
+        D((T, n // 2 - 1)), D((T, n // 2 - 1)), D((T, n // 2)), D((T, n // 2)),
+    ]
+    vm = pl.BlockSpec(memory_space=pltpu.VMEM)
+    hbm = pl.BlockSpec(memory_space=pl.ANY)
+    factors, loadings, fit = pl.pallas_call(
+        functools.partial(kernel, n),
+        out_shape=(
+            jax.ShapeDtypeStruct(cell_init.shape, f32),
+            jax.ShapeDtypeStruct(load_init.shape, f32),
+            jax.ShapeDtypeStruct((nb, 128), f32),
+        ),
+        in_specs=[pl.BlockSpec(memory_space=pltpu.SMEM), hbm, vm, vm, hbm],
+        out_specs=(vm, vm, vm),
+        scratch_shapes=scratch,
+        compiler_params=pltpu.CompilerParams(
+            collective_id=0, has_side_effects=True, vmem_limit_bytes=48 * 1024 * 1024
+        ),
+    )(band_offsets, counts, cell_init, load_init, band_weights)
+    return factors, loadings, fit.reshape(-1)
 
 
 def extended(cells, sides, width):
@@ -34,6 +450,9 @@
 
 
 def body(counts, cell_init, load_init, band_offsets, band_weights):
+    count = lax.axis_size("cell")
+    if count == 16 and load_init.shape == (64, 160) and counts.shape[0] == 128 * band_weights.shape[0]:
+        return fused(count, counts, cell_init, load_init, band_offsets, band_weights)
     highest = lax.Precision.HIGHEST
     factors = cell_init
     loadings = load_init

time: 355 us -> 70.7 us (0.20)
  blocking collectives: 278 us -> 0 us
  Pallas kernels: 0 us -> 63.8 us
  matrix products: 42.6 us -> 0 us
  between operations: 14.4 us -> 0.64 us
  starting transfers between devices: 8.91 us -> 0 us
    psum x4 -> x0, blocking collectives: 241 us -> none  [the longest x2 121 us: body(): factor_gram = lax.psum(local_gram, 'cell')]
    pallas_call x0 -> x1, Pallas kernels: none -> 63.8 us  [fused(): pl.pallas_call(functools.partial(kernel, n), out_shape=(jax.ShapeDtypeStr...]
    all_gather x2 -> x0, blocking collectives: 37.4 us -> none  [body(): lax.all_gather(loadings.astype(jnp.bfloat16), 'cell', axis=1, tiled=True)]
    dot_general x14 -> x0, matrix products: 33.4 us -> none  [the longest x2 14.6 us: body(): lax.dot_general(load_half, counts, (((1,), (1,)), ((), ())), preferred_el...]
    unnamed x1 -> x0, matrix products: 9.22 us -> none
    ppermute x4 -> x0, starting transfers between devices: 8.83 us -> none  [the longest x2 6.24 us: extended(): lax.ppermute(tail, axis, [(i, (i + 1) % count) for i in range(ends)])]
  transfers between devices with their start and end apart: 6 -> 0, of which waited for: 0 -> 0; matrix products, arithmetic and copies ran while one was open for 1% -> 0% of each run, Pallas kernels for 0% -> 0%
where the time goes in v1:
time: 70.7 us; the launch traced here: 70.5 us
  Pallas kernels  63.8 us (90%)
  local copies, waits for them, and re-layouts  6.07 us (9%)
    pallas_call x1, Pallas kernels, fused(): pl.pallas_call(functools.partial(kernel, n), out_shape=(jax.ShapeDtypeStr...  63.8 us
    unnamed x10, local copies, waits for them, and re-layouts  6.07 us

profile of v1, /device:TPU:0, one launch (start us, length us, event | category | flops | bytes accessed | tf_op | source)
XLA Modules:
  0.0 70.5 jit_solution(9113149505860840969)
XLA Ops:
  0.6 0.8 %copy.8.offs = s32[16,3]{1,0:T(8,128)S(1)} copy(s32[16,3]{0,1:T(4,128)} %param.8) | data formatting | bytes 384 | tf_op args[3]
  1.4 0.0 copy-start
  1.4 1.4 %copy-done = bf16[16,3,128,128]{3,2,1,0:T(8,128)(2,1)S(1)} copy-done((bf16[16,3,128,128]{3,2,1,0:T(8,128)(2,1)S(1)}, bf16[16,3,128,128]{3,2,1,0:T(8,128)(2,1)}, u32[]{:S(2)}) %copy-start) | copy-done | bytes 1572888
  2.8 0.0 copy-start.1
  2.8 1.0 %copy-done.1 = f32[64,2048]{1,0:T(8,128)S(1)} copy-done((f32[64,2048]{1,0:T(8,128)S(1)}, f32[64,2048]{1,0:T(8,128)}, u32[]{:S(2)}) %copy-start.1) | copy-done | bytes 524312
  3.8 0.0 copy-start.2
  3.8 0.8 %copy-done.2 = f32[64,160]{1,0:T(8,128)S(1)} copy-done((f32[64,160]{1,0:T(8,128)S(1)}, f32[64,160]{1,0:T(8,128)}, u32[]{:S(2)}) %copy-start.2) | copy-done | bytes 40984
  4.7 63.8 %shard_map.76 = (f32[64,2048]{1,0:T(8,128)S(1)}, f32[64,160]{1,0:T(8,128)S(1)}, f32[16,128]{1,0:T(8,128)S(1)}) custom-call(s32[16,3]{1,0:T(8,128)S(1)} %copy.8.offs, bf16[2048,2560]{1,0:T(8,128)(2,1)} %counts.1, f32[64,2048]{1,0:T(8,128)S(1)} %copy-done.1, f32[64,160]{1,0:T(8,128)S(1)} %copy-done.2, bf16[16,3,128,128]{3,2,1,0:T(8,128)(2,1)S(1)} %copy-done), custom_call_target="tpu_custom_call" | custom-call | tf_op jit(solution)/shard_map/pallas_call | solution.py:412
  68.5 0.8 %copy.12 = f32[64,2048]{1,0:T(8,128)} copy(f32[64,2048]{1,0:T(8,128)S(1)} %get-tuple-element.12) | data formatting | bytes 1048576
  69.2 0.6 copy.13
  69.9 0.6 copy.14
Async XLA Ops:
  1.4 1.4 %copy-start = (bf16[16,3,128,128]{3,2,1,0:T(8,128)(2,1)S(1)}, bf16[16,3,128,128]{3,2,1,0:T(8,128)(2,1)}, u32[]{:S(2)}) copy-start(bf16[16,3,128,128]{3,2,1,0:T(8,128)(2,1)} %weights.1) | copy-start | bytes 4718596
  2.8 1.0 %copy-start.1 = (f32[64,2048]{1,0:T(8,128)S(1)}, f32[64,2048]{1,0:T(8,128)}, u32[]{:S(2)}) copy-start(f32[64,2048]{1,0:T(8,128)} %cell_init.1) | copy-start | bytes 1572868
  3.8 0.8 %copy-start.2 = (f32[64,160]{1,0:T(8,128)S(1)}, f32[64,160]{1,0:T(8,128)}, u32[]{:S(2)}) copy-start(f32[64,160]{1,0:T(8,128)} %load_init.1) | copy-start | bytes 122884

commit v2 on v1

--- a/solution.py
+++ b/solution.py
@@ -105,11 +105,11 @@
 
 
 def kernel(
-    n, offs, counts, cell_init, load_init, weights, factors_out, load_out, fit_out,
-    cbuf, wbuf, fcur, xf, fb0, fb1, lcur, lhf, dt, gt, deg, csq,
-    fg_own, fg_got, fg_sum, fg_sib, lg_own, lg_got, lg_sum, lg_sib,
+    n, offs_in, counts, cell_in, load_in, weights, factors_out, load_out, fit_out,
+    offs, cell_init, load_init, cbuf, wbuf, fcur, xf, fb0, fb1, lcur, lhf, dt, gt, deg, csq,
+    fg_own, fg_got, lg_own, lg_got,
     a_buf, a_got, b_buf, b_got, c_buf, c_got, lh_all,
-    csem, wsem, halo_s, halo_r, g_s, g_r, gs_s, gs_r,
+    isem, csem, wsem, halo_s, halo_r, g_s, g_r,
     a_s, a_r, b_s, b_r, c_s, c_r, l_s, l_r, ls_s, ls_r,
 ):
     me = lax.axis_index("cell")
@@ -118,8 +118,6 @@
     z = lax.div(me, 4)
     sib = me + 1 - 2 * core
     ynb = me + 2 - 4 * y
-    line = lax.div(me, 2)
-    nline = n // 2
     nb = weights.shape[0]
     fbs = (fb0, fb1)
 
@@ -127,6 +125,12 @@
     for j in range(1, n):
         pl.semaphore_signal(barrier, inc=1, device_id={"cell": lax.rem(me + j, n)}, device_id_type=MESH)
 
+    icopies = [
+        pltpu.make_async_copy(src, dst, isem.at[i])
+        for i, (src, dst) in enumerate(((cell_in, cell_init), (load_in, load_init), (offs_in, offs)))
+    ]
+    for cp in icopies:
+        cp.start()
     width = 640
     chunk_at = [pl.multiple_of(lax.rem(z + o, n // 4) * width, width) for o in ORDER]
     ccopies = []
@@ -139,6 +143,8 @@
     wcopy = pltpu.make_async_copy(weights, wbuf, wsem)
     wcopy.start()
 
+    for cp in icopies:
+        cp.wait()
     lcur[...] = jnp.zeros_like(lcur)
     lcur[:, 0:160] = load_init[...]
     sends = []
@@ -209,25 +215,27 @@
             def _():
                 right.wait_send()
 
-    def gram_start(k, it, own, got, x):
-        own[it] = packed_gram(x)
+    def gram_send(k, it, own, got, step, x):
+        own[it, step] = x
+        if step < 2:
+            devs = [(sib, ynb)[step]]
+        else:
+            devs = [4 * lax.rem(z + o, 4) + 2 * y + core for o in (2, 1, 3)]
         return [
-            push(own.at[it], got.at[it, j - 1], g_s.at[k, it, j - 1], g_r.at[k, it, j - 1],
-                 2 * lax.rem(line + j, nline) + core)
-            for j in range(1, nline)
+            push(own.at[it, step], got.at[it, step + j], g_s.at[k, it, step + j], g_r.at[k, it, step + j], dev)
+            for j, dev in enumerate(devs)
         ]
 
-    def gram_middle(k, it, copies, own, got, total, far):
-        acc = own[it]
+    def gram_next(k, it, copies, own, got, step):
+        copies[0].wait_recv()
+        return gram_send(k, it, own, got, step, own[it, step - 1] + got[it, step - 1])
+
+    def gram_end(it, copies, own, got):
+        acc = own[it, 2]
         for j, cp in enumerate(copies):
             cp.wait_recv()
-            acc = acc + got[it, j]
-        total[it] = acc
-        return push(total.at[it], far.at[it], gs_s.at[k, it], gs_r.at[k, it], sib)
-
-    def gram_end(it, copy, total, far):
-        copy.wait_recv()
-        return gram_operand(total[it] + far[it])
+            acc = acc + got[it, 2 + j]
+        return gram_operand(acc)
 
     def graph(it, start, stop):
         fb = fbs[it]
@@ -262,7 +270,7 @@
     for it in range(ITERS):
         last = it == ITERS - 1
         halo(it, "start")
-        fgc = gram_start(0, it, fg_own, fg_got, xf[...])
+        fgc = gram_send(0, it, fg_own, fg_got, 0, packed_gram(xf[...]))
 
         acopies, bcopies, ccs = [], [], []
 
@@ -278,7 +286,6 @@
                 dev = 4 * lax.rem(z + ORDER[i], 4) + 2 * y + core
                 ccs.append(push(c_buf.at[it, i], c_got.at[it, i], c_s.at[it, i], c_r.at[it, i], dev))
 
-        fgm = None
         for i in range(4):
             if it == 0:
                 ccopies[i].wait()
@@ -292,8 +299,8 @@
                 reduce_core(i - 1)
             if i >= 2:
                 reduce_y(i - 2)
-            if i == 2:
-                fgm = gram_middle(0, it, fgc, fg_own, fg_got, fg_sum, fg_sib)
+            if i == 0 or i == 2:
+                fgc = gram_next(0, it, fgc, fg_own, fg_got, 1 + i // 2)
         if it == 0:
             wcopy.wait()
         halo(it, "recv")
@@ -302,7 +309,9 @@
         reduce_y(2)
         graph(it, nb // 4, nb // 2)
         reduce_y(3)
-        fg = gram_end(it, fgm, fg_sum, fg_sib)
+        graph(it, nb // 2, nb)
+        squares(it * nb // 2, it * nb // 2 + nb // 4)
+        fg = gram_end(it, fgc, fg_own, fg_got)
         own = lcur[...]
         lhi, llo = halves(own)
         under = dot(fg, jnp.concatenate([lhi, llo, lhi, llo], axis=0)) + epsilon
@@ -313,45 +322,65 @@
         own = own * unpack_piece(sums) / under
         lcur[...] = own
         lh_all[it, me] = pack_piece(own).astype(bf16)
-        lcs = [
-            push(lh_all.at[it, me], lh_all.at[it, me], l_s.at[it, j - 1], l_r.at[it, j - 1],
-                 2 * lax.rem(line + j, nline) + core)
-            for j in range(1, nline)
-        ]
-        sibs = [push(lh_all.at[it, me], lh_all.at[it, me], ls_s.at[it, 0], ls_r.at[it, 0], sib)]
+        def piece_of(o, t):
+            return 4 * lax.rem(z + 4 - o, 4) + 2 * (y if t == 0 else 1 - y) + core
+
+        def spread(o, t):
+            dev = 4 * lax.rem(z + o, 4) + 2 * (y if t == 0 else 1 - y) + core
+            m = 2 * o + t
+            lcs[m] = push(lh_all.at[it, me], lh_all.at[it, me], l_s.at[it, m - 1], l_r.at[it, m - 1], dev)
+
+        def hand_on(o, t):
+            m, at = 2 * o + t, piece_of(o, t)
+            if m:
+                pltpu.make_async_remote_copy(
+                    src_ref=lh_all.at[it, at], dst_ref=lh_all.at[it, at], send_sem=l_s.at[it, m - 1],
+                    recv_sem=l_r.at[it, m - 1], device_id={"cell": at}, device_id_type=MESH,
+                ).wait_recv()
+            sibs[m] = push(lh_all.at[it, at], lh_all.at[it, at], ls_s.at[it, m], ls_r.at[it, m], sib)
+
+        lcs, sibs = {}, {}
+        spread(0, 1)
+        hand_on(0, 0)
+        for o, t in ((1, 0), (3, 0), (1, 1), (3, 1), (2, 0), (2, 1)):
+            spread(o, t)
         lhi, llo = halves(own)
-        lgc = gram_start(1, it, lg_own, lg_got, jnp.concatenate([lhi, llo], axis=0))
+        lgc = gram_send(1, it, lg_own, lg_got, 0, packed_gram(jnp.concatenate([lhi, llo], axis=0)))
         if last:
             load_out[...] = own[:, 0:160]
-        graph(it, nb // 2, nb)
-        for j in range(1, nline):
-            at = 2 * lax.rem(line + nline - j, nline) + core
-            pltpu.make_async_remote_copy(
-                src_ref=lh_all.at[it, at], dst_ref=lh_all.at[it, at], send_sem=l_s.at[it, j - 1],
-                recv_sem=l_r.at[it, j - 1], device_id={"cell": at}, device_id_type=MESH,
-            ).wait_recv()
-            sibs.append(push(lh_all.at[it, at], lh_all.at[it, at], ls_s.at[it, j], ls_r.at[it, j], sib))
-        if last:
-            squares(0, nb)
-        for cp in sibs:
-            cp.wait_recv()
-        for c in range(n // 4):
+
+        def data(o):
+            for t in range(2):
+                sibs[2 * o + t].wait_recv()
+            c = lax.rem(z + 4 - o, 4)
             pieces = [lh_all[it, 4 * c + p].astype(f32) for p in range(4)]
-            for t, tile in enumerate(unpack_chunk(pieces)):
-                at = width * c + LANES * t
-                lhf[:, at : at + LANES] = tile.astype(bf16)
-
-        def data(i, carry):
-            rows = pl.ds(pl.multiple_of(i * 256, 256), 256)
-            part = dot_t(lhf[...], cbuf[rows, :])
-            dt[2 * i] = part[:, 0:LANES]
-            dt[2 * i + 1] = part[:, LANES:]
-            return carry
-
-        lax.fori_loop(0, nb // 4, data, 0)
-        lgm = gram_middle(1, it, lgc, lg_own, lg_got, lg_sum, lg_sib)
-        lax.fori_loop(nb // 4, nb // 2, data, 0)
-        lg = gram_end(it, lgm, lg_sum, lg_sib)
+            cols = pl.ds(pl.multiple_of(c * width, width), width)
+            lhf[:, cols] = jnp.concatenate(unpack_chunk(pieces), axis=1).astype(bf16)
+            tall = 512
+
+            def step(i, carry):
+                rows = pl.ds(pl.multiple_of(i * tall, tall), tall)
+                part = dot_t(cbuf[rows, cols], lhf[:, cols])
+                dt[rows, :] = part if o == 0 else dt[rows, :] + part
+                return carry
+
+            lax.fori_loop(0, nb * LANES // tall, step, 0)
+
+        squares(it * nb // 2 + nb // 4, (it + 1) * nb // 2)
+        hand_on(0, 1)
+        lgc = gram_next(1, it, lgc, lg_own, lg_got, 1)
+        hand_on(1, 0)
+        hand_on(1, 1)
+        data(0)
+        hand_on(3, 0)
+        hand_on(3, 1)
+        lgc = gram_next(1, it, lgc, lg_own, lg_got, 2)
+        data(1)
+        hand_on(2, 0)
+        hand_on(2, 1)
+        data(3)
+        data(2)
+        lg = gram_end(it, lgc, lg_own, lg_got)
         if last:
             twice = dot_t(lhf[...], jnp.concatenate([lhf[...], lhf[...]], axis=0))
             mhi, mlo = halves(twice)
@@ -360,23 +389,34 @@
         source = cell_init if it == 0 else fcur
         target = factors_out if last else fcur
 
-        def update(b, carry):
-            cols = pl.ds(pl.multiple_of(b * LANES, LANES), LANES)
-            f = source[:, cols]
+        def update(pair_at, carry):
+            cols = pl.ds(pl.multiple_of(pair_at * 2 * LANES, 2 * LANES), 2 * LANES)
             x = xf[:, cols]
-            under = dot(lg, jnp.concatenate([x, x], axis=0)) + deg[b][0:1] * f + epsilon
-            new = f * (dt[b] + gt[b]) / under
-            target[:, cols] = new
+            product = dot(lg, jnp.concatenate([x, x], axis=0))
+            news, datas = [], []
+            for h in range(2):
+                b = 2 * pair_at + h
+                at = pl.ds(pl.multiple_of(b * LANES, LANES), LANES)
+                f = source[:, at]
+                data_term = dt[at, :].T
+                under = product[:, h * LANES : (h + 1) * LANES] + deg[b][0:1] * f + epsilon
+                new = f * (data_term + gt[b]) / under
+                target[:, at] = new
+                news.append(new)
+                datas.append(data_term)
+                if not last:
+                    set_factors(it + 1, b, new)
             if last:
-                hi = new.astype(bf16)
-                recon2 = dot(pair, jnp.concatenate([hi, hi], axis=0))
-                inner = jnp.sum(hi.astype(f32) * (recon2 - 2.0 * dt[b]), axis=0, keepdims=True)
-                fit_out[pl.ds(b, 1), :] = (csq[b][0:1] + inner) * (1.0 / cbuf.shape[1])
-            else:
-                set_factors(it + 1, b, new)
+                hi = jnp.concatenate(news, axis=1).astype(bf16)
+                recon2 = dot(pair, jnp.concatenate([hi, hi], axis=0)) - 2.0 * jnp.concatenate(datas, axis=1)
+                inner = jnp.sum(hi.astype(f32) * recon2, axis=0, keepdims=True)
+                for h in range(2):
+                    b = 2 * pair_at + h
+                    total = csq[b][0:1] + inner[:, h * LANES : (h + 1) * LANES]
+                    fit_out[pl.ds(b, 1), :] = total * (1.0 / cbuf.shape[1])
             return carry
 
-        lax.fori_loop(0, nb, update, 0, unroll=2)
+        lax.fori_loop(0, nb // 2, update, 0, unroll=2)
 
     for cp in sends:
         cp.wait_send()
@@ -391,19 +431,20 @@
     V = pltpu.VMEM
     D = pltpu.SemaphoreType.DMA
     scratch = [
+        pltpu.SMEM(band_offsets.shape, jnp.int32), V((64, cells), f32), V((64, 160), f32),
         V((cells, genes), bf16), V(band_weights.shape, bf16), V((64, cells), f32), V((128, cells), bf16),
         V((nb + 4, 64, 128), bf16), V((nb + 4, 64, 128), bf16), V((64, 256), f32), V((64, genes), bf16),
-        V((nb, 64, 128), f32), V((nb, 64, 128), f32), V((nb, 8, 128), f32), V((nb, 8, 128), f32),
+        V((cells, 64), f32), V((nb, 64, 128), f32), V((nb, 8, 128), f32), V((nb, 8, 128), f32),
     ]
     for _ in range(2):
-        scratch += [V((T, 32, 128), f32), V((T, n // 2 - 1, 32, 128), f32), V((T, 32, 128), f32), V((T, 32, 128), f32)]
+        scratch += [V((T, 3, 32, 128), f32), V((T, 5, 32, 128), f32)]
     scratch += [
         V((T, 4, 2, 2, 80, 128), f32), V((T, 4, 2, 80, 128), f32),
         V((T, 4, 2, 80, 128), f32), V((T, 4, 80, 128), f32),
         V((T, 4, 80, 128), f32), V((T, 3, 80, 128), f32),
         V((T, n, 80, 128), bf16),
-        D((4,)), D(()), D((T, 2)), D((T, 2)),
-        D((2, T, n // 2 - 1)), D((2, T, n // 2 - 1)), D((2, T)), D((2, T)),
+        D((3,)), D((4,)), D(()), D((T, 2)), D((T, 2)),
+        D((2, T, 5)), D((2, T, 5)),
         D((T, 4)), D((T, 4)), D((T, 4)), D((T, 4)), D((T, 3)), D((T, 3)),
         D((T, n // 2 - 1)), D((T, n // 2 - 1)), D((T, n // 2)), D((T, n // 2)),
     ]
@@ -416,7 +457,7 @@
             jax.ShapeDtypeStruct(load_init.shape, f32),
             jax.ShapeDtypeStruct((nb, 128), f32),
         ),
-        in_specs=[pl.BlockSpec(memory_space=pltpu.SMEM), hbm, vm, vm, hbm],
+        in_specs=[hbm] * 5,
         out_specs=(vm, vm, vm),
         scratch_shapes=scratch,
         compiler_params=pltpu.CompilerParams(

time: 70.7 us -> 64.8 us (0.917)
  Pallas kernels: 63.8 us -> 57.8 us
    pallas_call x1, Pallas kernels: 63.8 us -> 57.8 us  [fused(): pl.pallas_call(functools.partial(kernel, n), out_shape=(jax.ShapeDtypeStr...]
where the time goes in v2:
time: 64.8 us; the launch traced here: 64.6 us
  Pallas kernels  57.8 us (89%)
  local copies, waits for them, and re-layouts  6.07 us (9%)
    pallas_call x1, Pallas kernels, fused(): pl.pallas_call(functools.partial(kernel, n), out_shape=(jax.ShapeDtypeStr...  57.8 us
    unnamed x10, local copies, waits for them, and re-layouts  6.07 us

profile of v2, /device:TPU:0, one launch (start us, length us, event | category | flops | bytes accessed | tf_op | source)
XLA Modules:
  0.0 64.6 jit_solution(8934149702246749698)
XLA Ops:
  0.6 0.8 %copy.8.offs_in = s32[16,3]{1,0:T(8,128)S(1)} copy(s32[16,3]{0,1:T(4,128)} %param.8) | data formatting | bytes 384 | tf_op args[3]
  1.4 0.0 copy-start
  1.4 1.4 %copy-done = bf16[16,3,128,128]{3,2,1,0:T(8,128)(2,1)S(1)} copy-done((bf16[16,3,128,128]{3,2,1,0:T(8,128)(2,1)S(1)}, bf16[16,3,128,128]{3,2,1,0:T(8,128)(2,1)}, u32[]{:S(2)}) %copy-start) | copy-done | bytes 1572888
  2.8 0.0 copy-start.1
  2.8 1.0 %copy-done.1 = f32[64,2048]{1,0:T(8,128)S(1)} copy-done((f32[64,2048]{1,0:T(8,128)S(1)}, f32[64,2048]{1,0:T(8,128)}, u32[]{:S(2)}) %copy-start.1) | copy-done | bytes 524312
  3.8 0.0 copy-start.2
  3.8 0.8 %copy-done.2 = f32[64,160]{1,0:T(8,128)S(1)} copy-done((f32[64,160]{1,0:T(8,128)S(1)}, f32[64,160]{1,0:T(8,128)}, u32[]{:S(2)}) %copy-start.2) | copy-done | bytes 40984
  4.7 57.8 %shard_map.76 = (f32[64,2048]{1,0:T(8,128)S(1)}, f32[64,160]{1,0:T(8,128)S(1)}, f32[16,128]{1,0:T(8,128)S(1)}) custom-call(s32[16,3]{1,0:T(8,128)S(1)} %copy.8.offs_in, bf16[2048,2560]{1,0:T(8,128)(2,1)} %counts.1, f32[64,2048]{1,0:T(8,128)S(1)} %copy-done.1, f32[64,160]{1,0:T(8,128)S(1)} %copy-done.2, bf16[16,3,128,128]{3,2,1,0:T(8,128)(2,1)S(1)} %copy-done), custom_call_target="tpu_custom_call" | custom-call | tf_op jit(solution)/shard_map/pallas_call | solution.py:453
  62.5 0.8 %copy.12 = f32[64,2048]{1,0:T(8,128)} copy(f32[64,2048]{1,0:T(8,128)S(1)} %get-tuple-element.12) | data formatting | bytes 1048576
  63.3 0.6 copy.13
  64.0 0.6 copy.14
Async XLA Ops:
  1.4 1.4 %copy-start = (bf16[16,3,128,128]{3,2,1,0:T(8,128)(2,1)S(1)}, bf16[16,3,128,128]{3,2,1,0:T(8,128)(2,1)}, u32[]{:S(2)}) copy-start(bf16[16,3,128,128]{3,2,1,0:T(8,128)(2,1)} %weights.1) | copy-start | bytes 4718596
  2.8 1.0 %copy-start.1 = (f32[64,2048]{1,0:T(8,128)S(1)}, f32[64,2048]{1,0:T(8,128)}, u32[]{:S(2)}) copy-start(f32[64,2048]{1,0:T(8,128)} %cell_in.1) | copy-start | bytes 1572868
  3.8 0.8 %copy-start.2 = (f32[64,160]{1,0:T(8,128)S(1)}, f32[64,160]{1,0:T(8,128)}, u32[]{:S(2)}) copy-start(f32[64,160]{1,0:T(8,128)} %load_in.1) | copy-start | bytes 122884
